TPU v7x, 128 devices: a whole 4x4x4 slice. The times are simulated.
128 devices in a mesh: gx: 8 (over y, z_hi), gy: 4 (over x), gz: 4 (over z_lo, core).
Axes of the slice: x: 4, y: 4, z: 4 (z_hi: 2, z_lo: 2; z = z_hi * 2 + z_lo), core: 2. Of those that a mesh axis runs over, the one named last changes fastest.
Arguments:
- field_window: float32 [16, 32, 1024, 1024], P('gx', None, 'gy', 'gz'), may hold values from -54 to 54
- second_factor: float32 [1024, 64], P('gy'), may hold values from -1 to 1
- third_factor: float32 [1024, 64], P('gz'), may hold values from -1 to 1
- species_factor: float32 [32, 8], replicated, may hold values from -3 to 3
Outputs:
- core_tensor: float32 [64, 64, 16, 8], P('gy', 'gz', 'gx')
- mode_gram: float32 [16, 16], P('gx')
All inputs are finite; a program needn't handle non-finite values.
Results may differ from a plain program's by a relative error of at most 0.00007.
Values sent between devices are 32-bit elements; how exact they have to be, the bound alone decides.
No kernel may reach another device: no remote copies, remote signals or barrier semaphores. Data moves between devices by JAX's collectives and lax.ppermute only.
A program may use at most 64 MiB of HBM per device.

v0:
```python
import jax
import jax.numpy as jnp
from jax import lax
from jax.experimental import pallas as pl
from jax.experimental.pallas import tpu as pltpu
from jax.sharding import PartitionSpec as P

HIGHEST = lax.Precision.HIGHEST
F32 = jnp.float32
BF16 = jnp.bfloat16
AXES = ("gx", "gy", "gz")
ROWS = 64
REGION = 64


def split(v):
    high = v.astype(BF16)
    return high, (v - high.astype(F32)).astype(BF16)


def dot(a, b):
    return jnp.dot(a, b, preferred_element_type=F32)


def mask(shape, f):
    i = lax.broadcasted_iota(jnp.int32, shape, 0)
    j = lax.broadcasted_iota(jnp.int32, shape, 1)
    return jnp.where(f(i, j), 1.0, 0.0).astype(F32)


def project_kernel(
    field, second_hbm, third_hbm, species_hbm, out, window, spread, v_both, high, low,
    second, third, species, sems, factor_sems,
):
    planes, count, rows, columns = field.shape
    per = rows // ROWS

    def copy(c):
        p, k = c // per, c % per
        return pltpu.make_async_copy(
            field.at[p, :, pl.ds(k * ROWS, ROWS), :], window.at[c], sems.at[c]
        )

    factors = [
        pltpu.make_async_copy(source, target, factor_sems.at[i])
        for i, (source, target) in enumerate(
            ((species_hbm, species), (second_hbm, second), (third_hbm, third))
        )
    ]
    for factor in factors:
        factor.start()
    for c in range(2):
        copy(c).start()
    for factor in factors:
        factor.wait()
    for c in range(2, planes * per):
        copy(c).start()
    x = lax.axis_index("gy")
    given = lax.axis_index("gz") // 2 ^ lax.axis_index("gz") % 2 ^ lax.axis_index("gx") % 2

    r_of = mask((64, 8), lambda i, j: i // 8 == j)
    s_of = mask((32, 256), lambda i, j: j // 8 == i)
    w = jnp.dot(jnp.dot(r_of, species[...], precision=HIGHEST), s_of, precision=HIGHEST)
    w_high, w_low = split(w * mask((64, 256), lambda i, j: i % 8 == j % 8))
    spread[0:64] = w_high
    spread[64:128] = w_low

    def rank_second(i):
        return (x + i // 16) % 4 * 16 + i % 16

    u = jnp.dot(mask((64, 64), lambda i, j: rank_second(i) == j), second[...], precision=HIGHEST)
    u_high, u_low = split(u)
    u_both = jnp.concatenate([u_high, u_low], axis=0)

    pick = mask((256, 64), lambda i, j: j == (given ^ i // 128) * 32 + i % 32)
    v = lax.dot_general(third[...], pick, (((0,), (1,)), ((), ())), precision=HIGHEST)
    v_both[0], v_both[1] = split(v)
    lane = lax.broadcasted_iota(jnp.int32, (64, 256), 1) % 128 // 32

    for p in range(planes):

        def step(k, carry, p=p):
            first = p * per + k * (REGION // ROWS)
            for c in range(REGION // ROWS):
                copy(first + c).wait()
            w_both = spread[...]
            for g in range(REGION // 16):
                parts = []
                for h in range(2):
                    at = g * 16 + h * 8
                    f = window[first + at // ROWS, :, at % ROWS : at % ROWS + 8, :]
                    f_high, f_low = split(f.reshape(count * 8, columns))
                    d = dot(w_both, f_high)
                    d = d[:64] + d[64:] + dot(w_both[:64], f_low)
                    parts.append(d.reshape(8, 8, columns))
                r_high, r_low = split(jnp.concatenate(parts, axis=1))
                at = pl.ds(pl.multiple_of(k * REGION + g * 16, 16), 16)
                high[:, at, :] = r_high
                low[:, at, :] = r_low
            return carry

        lax.fori_loop(0, rows // REGION, step, 0)
        ts = []
        for r in range(8):
            d = dot(u_both, high[r])
            ts.append(d[:64] + d[64:] + dot(u_both[:64], low[r]))
        t_high, t_low = split(jnp.concatenate(ts, axis=0))
        e = dot(jnp.concatenate([t_high, t_low], axis=0), v_both[0])
        e = (e[:512] + e[512:] + dot(t_high, v_both[1])).reshape(8, 64, 256)
        for half in range(2):
            total = e[half * 4]
            for q in range(1, 4):
                total = jnp.where(lane == q, e[half * 4 + q], total)
            for zs in range(2):
                for xs in range(4):
                    at = zs * 256 + xs * 64 + p * 32 + half * 16
                    out[at : at + 16, :] = total[xs * 16 : xs * 16 + 16, zs * 128 : zs * 128 + 128]


def project(field, second, third, species):
    planes, count, rows, columns = field.shape
    vmem = pl.BlockSpec(memory_space=pltpu.VMEM)
    pieces = planes * rows // ROWS
    return pl.pallas_call(
        project_kernel,
        out_shape=pltpu.VMEM((512, 128), F32),
        in_specs=[pl.BlockSpec(memory_space=pltpu.HBM)] * 4,
        out_specs=vmem,
        scratch_shapes=[
            pltpu.VMEM((pieces, count, ROWS, columns), F32),
            pltpu.VMEM((128, 256), BF16),
            pltpu.VMEM((2, columns, 256), BF16),
            pltpu.VMEM((8, rows, columns), BF16),
            pltpu.VMEM((8, rows, columns), BF16),
            pltpu.VMEM(second.shape, F32),
            pltpu.VMEM(third.shape, F32),
            pltpu.VMEM(species.shape, F32),
            pltpu.SemaphoreType.DMA((pieces,)),
            pltpu.SemaphoreType.DMA((3,)),
        ],
        compiler_params=pltpu.CompilerParams(vmem_limit_bytes=48 << 20),
        cost_estimate=pl.CostEstimate(
            flops=1 << 32, bytes_accessed=17 << 20, transcendentals=0
        ),
    )(field, *[pltpu.with_memory_space_constraint(v, pltpu.HBM) for v in (second, third, species)])


def gram_kernel(three, mine, two, one, out):
    gx = lax.axis_index("gx")
    y, h = gx // 2, gx % 2
    sums = []
    for p in range(2):
        own = mine[64 + p * 32 : 96 + p * 32, :]
        for ref in (mine, one, two, three):
            for m in range(4):
                product = own * ref[m * 32 : m * 32 + 32, :]
                sums.append(product[0:8] + product[8:16] + product[16:24] + product[24:32])
    sums = jnp.sum(jnp.concatenate(sums, axis=0), axis=1, keepdims=True)
    row = lax.broadcasted_iota(jnp.int32, (256, 128), 0) // 8 % 16
    lane = lax.broadcasted_iota(jnp.int32, (256, 128), 1)
    plane = ((y - row // 4) % 4 * 2 + (h ^ (1 - row // 2 % 2))) * 2 + row % 2
    placed = jnp.where(lane == plane, sums, 0.0)
    rows = [jnp.sum(placed[p * 128 : p * 128 + 128], axis=0, keepdims=True) for p in range(2)]
    rows.append(jnp.zeros((6, 128), F32))
    out[...] = jnp.concatenate(rows, axis=0) * (1.0 / 32768.0)


def gram(*blocks):
    vmem = pl.BlockSpec(memory_space=pltpu.VMEM)
    return pl.pallas_call(
        gram_kernel,
        out_shape=jax.ShapeDtypeStruct((8, 128), F32),
        in_specs=[vmem] * 4,
        out_specs=vmem,
        compiler_params=pltpu.CompilerParams(vmem_limit_bytes=4 << 20),
        cost_estimate=pl.CostEstimate(flops=1 << 20, bytes_accessed=1 << 18, transcendentals=0),
    )(*blocks)


def arrange_kernel(here, there, out):
    core = lax.axis_index("gz") % 2
    block = jnp.where(lax.axis_index("gx") % 2 == 0, here[...], there[...])
    block = jnp.where(core == 1, pltpu.roll(block, 112, 1), block)
    for p in range(2):
        for half in range(2):
            at = p * 32 + half * 16
            for q in range(4):
                out[:, p, half * 4 + q, :] = block[at : at + 16, q * 32 : q * 32 + 16]


def arrange(here, there):
    vmem = pl.BlockSpec(memory_space=pltpu.VMEM)
    return pl.pallas_call(
        arrange_kernel,
        out_shape=jax.ShapeDtypeStruct((16, 2, 8, 16), F32),
        in_specs=[vmem, vmem],
        out_specs=vmem,
        compiler_params=pltpu.CompilerParams(vmem_limit_bytes=4 << 20),
        cost_estimate=pl.CostEstimate(flops=1 << 16, bytes_accessed=1 << 18, transcendentals=0),
    )(here, there)


CHIPS = [(y, h, x, z) for y in range(4) for h in range(2) for x in range(4) for z in range(2)]


def index(y, h, x, z, core):
    return (y * 2 + h) * 16 + x * 4 + z * 2 + core


def swap(v):
    pairs = [(index(*chip, c), index(*chip, 1 - c)) for chip in CHIPS for c in range(2)]
    return lax.ppermute(v, AXES, pairs)


def send(v, core, to):
    pairs = []
    for chip in CHIPS:
        pairs.append((index(*chip, core), index(*to(*chip), 1 - core)))
        pairs.append((index(*chip, 1 - core), index(*chip, core)))
    return lax.ppermute(v, AXES, pairs)


def trade(v):
    pairs = [(index(*chip, c), index(*over_z(*chip), c)) for chip in CHIPS for c in range(2)]
    return lax.ppermute(v, AXES, pairs)


def together(*values):
    return lax.optimization_barrier(values)


def over_z(y, h, x, z):
    return y, h, x, 1 - z


def over_h(y, h, x, z):
    return y, 1 - h, x, 1 - z


def over_x(k):
    return lambda y, h, x, z: (y, h, (x + k) % 4, z)


def over_y(k):
    return lambda y, h, x, z: ((y + k) % 4, h, x, z)


def on_device(field_window, second_factor, third_factor, species_factor):
    part = project(field_window, second_factor.T, third_factor.T, species_factor.T)
    first_core = lax.axis_index("gz") % 2 == 0
    with jax.named_scope("reduce"):
        part = part[256:] + swap(part[:256])
        part = send(part, 0, over_z) + part
        terms = [send(part[64 * k : 64 * k + 64], 1, over_x(k)) for k in (2, 1, 3)]
        terms = together(*terms, swap(part[:64]))
        block = ((terms[0] + terms[1]) + terms[2]) + terms[3]
    with jax.named_scope("gather"):
        far, mine = together(send(block, 0, over_h), swap(block))
        near = jnp.concatenate([far, mine])
        two, one, three = [send(near, 1, over_y(k)) for k in (2, 1, 3)]
        near = swap(near)
    with jax.named_scope("gram"):
        total = gram(three, near, two, one)
        total, here = together(total, jnp.where(first_core, block, mine))
        there = trade(here)
        terms = [send(total, 0, over_x(k)) for k in (2, 1, 3)]
        terms = together(*terms, swap(total))
        total = ((terms[0] + terms[1]) + terms[2]) + terms[3]
        arranged = arrange(here, there)
        other, far, mine, arranged = together(
            trade(total), send(total, 1, over_z), swap(total), arranged
        )
        mode_gram = jnp.where(first_core, far + mine, total + other)[:2, :16]
    return (jnp.transpose(arranged, (0, 3, 1, 2)), mode_gram)


def solution(mesh):
    in_specs = (P("gx", None, "gy", "gz"), P("gy", None), P("gz", None), P())
    out_specs = (P("gy", "gz", "gx", None), P("gx", None))
    return jax.shard_map(
        on_device, mesh=mesh, in_specs=in_specs, out_specs=out_specs, check_vma=False
    )
```

profile of v0, /device:TPU:1, one launch (start us, length us, event | category | flops | bytes accessed | tf_op | source)
XLA Modules:
  0.0 40.8 jit_solution(9756277564851868086)
XLA Ops:
  0.6 8.1 %shard_map.59 = f32[512,128]{1,0:T(8,128)S(1)} custom-call(f32[2,32,256,256]{3,2,1,0:T(8,128)} %field.1, f32[64,256]{1,0:T(8,128)} %bitcast.5, f32[64,256]{1,0:T(8,128)} %bitcast.6, f32[8,32]{1,0:T(8,128)} %bitcast.7), custom_call_target="tpu_custom_call" | custom-call | flops 4294967296 | bytes 17825792 | tf_op jit(solution)/shard_map/pallas_call | solution.py:124
  8.8 1.5 %collective-permute-start = (f32[256,128]{1,0:T(8,128)S(1)}, f32[256,128]{1,0:T(8,128)S(1)}, u32[]{:S(2)}, u32[]{:S(2)}) collective-permute-start(f32[256,128]{1,0:T(8,128)S(1)} %slice.29), channel_id=1, source_target_pairs={{0,1},{1,0},{2,3},{3,2},{4,5},{5,4},{6,7},{7,6},{8,9},{9,8},{10,11... | collective-permute-start | bytes 393224 | tf_op jit(solution)/shard_map/reduce/ppermute | solution.py:212
  10.3 1.0 %collective-permute-done = f32[256,128]{1,0:T(8,128)S(1)} collective-permute-done((f32[256,128]{1,0:T(8,128)S(1)}, f32[256,128]{1,0:T(8,128)S(1)}, u32[]{:S(2)}, u32[]{:S(2)}) %collective-permute-start) | collective-permute-done | bytes 131104 | tf_op jit(solution)/shard_map/reduce/ppermute | solution.py:212
  11.3 0.4 %collective-permute-start.1 = (f32[256,128]{1,0:T(8,128)S(1)}, f32[256,128]{1,0:T(8,128)S(1)}, u32[]{:S(2)}, u32[]{:S(2)}) collective-permute-start(f32[256,128]{1,0:T(8,128)S(1)} %slice_add_fusion), channel_id=1, source_target_pairs={{0,3},{1,0},{2,1},{3,2},{4,7},{5,4},{6,5},{7,6},{8,11},{9,8},{10,9... | collective-permute-start | bytes 393224 | tf_op jit(solution)/shard_map/reduce/ppermute | solution.py:220
  11.7 4.2 %collective-permute-done.1 = f32[256,128]{1,0:T(8,128)S(1)} collective-permute-done((f32[256,128]{1,0:T(8,128)S(1)}, f32[256,128]{1,0:T(8,128)S(1)}, u32[]{:S(2)}, u32[]{:S(2)}) %collective-permute-start.1) | collective-permute-done | bytes 131104 | tf_op jit(solution)/shard_map/reduce/ppermute | solution.py:220
  16.0 2.7 %collective-permute-start.2 = (f32[64,128]{1,0:T(8,128)S(1)}, f32[64,128]{1,0:T(8,128)S(1)}, u32[]{:S(2)}, u32[]{:S(2)}) collective-permute-start(f32[64,128]{1,0:T(8,128)S(1)} %get-tuple-element.37), channel_id=1, source_target_pairs={{1,8},{0,1},{3,10},{2,3},{5,12},{4,5},{7,14},{6,7},{9,0},{8,9},{11... | collective-permute-start | bytes 98312 | tf_op jit(solution)/shard_map/reduce/ppermute | solution.py:220
  18.7 0.0 collective-permute-start.3
  18.7 1.3 %collective-permute-start.4 = (f32[64,128]{1,0:T(8,128)S(1)}, f32[64,128]{1,0:T(8,128)S(1)}, u32[]{:S(2)}, u32[]{:S(2)}) collective-permute-start(f32[64,128]{1,0:T(8,128)S(1)} %get-tuple-element.35), channel_id=1, source_target_pairs={{1,12},{0,1},{3,14},{2,3},{5,0},{4,5},{7,2},{6,7},{9,4},{8,9},{11,... | collective-permute-start | bytes 98312 | tf_op jit(solution)/shard_map/reduce/ppermute | solution.py:220
  20.0 0.0 collective-permute-start.5
  20.0 0.0 collective-permute-done.2
  20.0 0.1 collective-permute-done.3
  20.1 1.0 %collective-permute-done.4 = f32[64,128]{1,0:T(8,128)S(1)} collective-permute-done((f32[64,128]{1,0:T(8,128)S(1)}, f32[64,128]{1,0:T(8,128)S(1)}, u32[]{:S(2)}, u32[]{:S(2)}) %collective-permute-start.4) | collective-permute-done | bytes 32800 | tf_op jit(solution)/shard_map/reduce/ppermute | solution.py:220
  21.0 0.2 collective-permute-done.5
  21.2 1.4 %collective-permute-start.6 = (f32[64,128]{1,0:T(8,128)S(1)}, f32[64,128]{1,0:T(8,128)S(1)}, u32[]{:S(2)}, u32[]{:S(2)}) collective-permute-start(f32[64,128]{1,0:T(8,128)S(1)} %add_add_fusion), channel_id=1, source_target_pairs={{0,19},{1,0},{2,17},{3,2},{4,23},{5,4},{6,21},{7,6},{8,27},{9,8},{... | collective-permute-start | bytes 98312 | tf_op jit(solution)/shard_map/gather/ppermute | solution.py:220
  22.7 1.6 %collective-permute-start.7 = (f32[64,128]{1,0:T(8,128)S(1)}, f32[64,128]{1,0:T(8,128)S(1)}, u32[]{:S(2)}, u32[]{:S(2)}) collective-permute-start(f32[64,128]{1,0:T(8,128)S(1)} %add_add_fusion), channel_id=1, source_target_pairs={{0,1},{1,0},{2,3},{3,2},{4,5},{5,4},{6,7},{7,6},{8,9},{9,8},{10,11... | collective-permute-start | bytes 98312 | tf_op jit(solution)/shard_map/gather/ppermute | solution.py:212
  24.3 2.1 %collective-permute-done.6 = f32[64,128]{1,0:T(8,128)S(1)} collective-permute-done((f32[64,128]{1,0:T(8,128)S(1)}, f32[64,128]{1,0:T(8,128)S(1)}, u32[]{:S(2)}, u32[]{:S(2)}) %collective-permute-start.6) | collective-permute-done | bytes 32800 | tf_op jit(solution)/shard_map/gather/ppermute | solution.py:220
  26.4 0.0 collective-permute-done.7
  26.4 2.4 %collective-permute-start.10 = (f32[128,128]{1,0:T(8,128)S(1)}, f32[128,128]{1,0:T(8,128)S(1)}, u32[]{:S(2)}, u32[]{:S(2)}) collective-permute-start(f32[128,128]{1,0:T(8,128)S(1)} %get-tuple-element.39), channel_id=1, source_target_pairs={{1,64},{0,1},{3,66},{2,3},{5,68},{4,5},{7,70},{6,7},{9,72},{8,9},{... | collective-permute-start | bytes 196616 | tf_op jit(solution)/shard_map/gather/ppermute | solution.py:220
  28.8 0.0 collective-permute-start.11
  28.8 1.1 %collective-permute-start.8 = (f32[128,128]{1,0:T(8,128)S(1)}, f32[128,128]{1,0:T(8,128)S(1)}, u32[]{:S(2)}, u32[]{:S(2)}) collective-permute-start(f32[128,128]{1,0:T(8,128)S(1)} %get-tuple-element.39), channel_id=1, source_target_pairs={{1,96},{0,1},{3,98},{2,3},{5,100},{4,5},{7,102},{6,7},{9,104},{8,9... | collective-permute-start | bytes 196616 | tf_op jit(solution)/shard_map/gather/ppermute | solution.py:220
  29.9 0.0 collective-permute-start.9
  29.9 0.2 collective-permute-done.10.two
  30.1 0.6 %collective-permute-done.11.one = f32[128,128]{1,0:T(8,128)S(1)} collective-permute-done((f32[128,128]{1,0:T(8,128)S(1)}, f32[128,128]{1,0:T(8,128)S(1)}, u32[]{:S(2)}, u32[]{:S(2)}) %collective-permute-start.11) | collective-permute-done | bytes 65568 | tf_op jit(solution)/shard_map/gather/ppermute | solution.py:220
  30.7 0.5 %collective-permute-done.8.three = f32[128,128]{1,0:T(8,128)S(1)} collective-permute-done((f32[128,128]{1,0:T(8,128)S(1)}, f32[128,128]{1,0:T(8,128)S(1)}, u32[]{:S(2)}, u32[]{:S(2)}) %collective-permute-start.8) | collective-permute-done | bytes 65568 | tf_op jit(solution)/shard_map/gather/ppermute | solution.py:220
  31.3 0.0 collective-permute-done.9.mine
  31.3 0.2 gram.2
  31.5 1.8 %collective-permute-start.12 = (f32[8,128]{1,0:T(8,128)S(1)}, f32[8,128]{1,0:T(8,128)S(1)}, u32[]{:S(2)}, u32[]{:S(2)}) collective-permute-start(f32[8,128]{1,0:T(8,128)S(1)} %gram.2), channel_id=1, source_target_pairs={{0,9},{1,0},{2,11},{3,2},{4,13},{5,4},{6,15},{7,6},{8,1},{9,8},{10... | collective-permute-start | bytes 12296 | tf_op jit(solution)/shard_map/gram/ppermute | solution.py:220
  33.3 0.1 collective-permute-start.13
  33.4 0.5 %collective-permute-start.14 = (f32[8,128]{1,0:T(8,128)S(1)}, f32[8,128]{1,0:T(8,128)S(1)}, u32[]{:S(2)}, u32[]{:S(2)}) collective-permute-start(f32[8,128]{1,0:T(8,128)S(1)} %gram.2), channel_id=1, source_target_pairs={{0,13},{1,0},{2,15},{3,2},{4,1},{5,4},{6,3},{7,6},{8,5},{9,8},{10,... | collective-permute-start | bytes 12296 | tf_op jit(solution)/shard_map/gram/ppermute | solution.py:220
  33.9 1.8 %collective-permute-start.15 = (f32[8,128]{1,0:T(8,128)S(1)}, f32[8,128]{1,0:T(8,128)S(1)}, u32[]{:S(2)}, u32[]{:S(2)}) collective-permute-start(f32[8,128]{1,0:T(8,128)S(1)} %gram.2), channel_id=1, source_target_pairs={{0,1},{1,0},{2,3},{3,2},{4,5},{5,4},{6,7},{7,6},{8,9},{9,8},{10,11... | collective-permute-start | bytes 12296 | tf_op jit(solution)/shard_map/gram/ppermute | solution.py:212
  35.7 0.3 collective-permute-start.19
  36.0 0.1 collective-permute-done.12
  36.1 1.4 %collective-permute-done.13 = f32[8,128]{1,0:T(8,128)S(1)} collective-permute-done((f32[8,128]{1,0:T(8,128)S(1)}, f32[8,128]{1,0:T(8,128)S(1)}, u32[]{:S(2)}, u32[]{:S(2)}) %collective-permute-start.13) | collective-permute-done | bytes 4128 | tf_op jit(solution)/shard_map/gram/ppermute | solution.py:220
  37.5 0.0 collective-permute-done.14
  37.5 0.0 collective-permute-done.15
  37.5 0.4 %collective-permute-start.16 = (f32[8,128]{1,0:T(8,128)S(1)}, f32[8,128]{1,0:T(8,128)S(1)}, u32[]{:S(2)}, u32[]{:S(2)}) collective-permute-start(f32[8,128]{1,0:T(8,128)S(1)} %add_add_fusion.1), channel_id=1, source_target_pairs={{0,2},{1,3},{2,0},{3,1},{4,6},{5,7},{6,4},{7,5},{8,10},{9,11},{10,... | collective-permute-start | bytes 12296 | tf_op jit(solution)/shard_map/gram/ppermute | solution.py:225
  38.0 0.7 %collective-permute-start.17 = (f32[8,128]{1,0:T(8,128)S(1)}, f32[8,128]{1,0:T(8,128)S(1)}, u32[]{:S(2)}, u32[]{:S(2)}) collective-permute-start(f32[8,128]{1,0:T(8,128)S(1)} %add_add_fusion.1), channel_id=1, source_target_pairs={{1,2},{0,1},{3,0},{2,3},{5,6},{4,5},{7,4},{6,7},{9,10},{8,9},{11,8... | collective-permute-start | bytes 12296 | tf_op jit(solution)/shard_map/gram/ppermute | solution.py:220
  38.6 0.0 collective-permute-start.18
  38.6 0.0 collective-permute-done.19.there
  38.7 1.0 %gram.3 = f32[16,2,8,16]{3,2,1,0:T(8,128)} custom-call(f32[64,128]{1,0:T(8,128)S(1)} %get-tuple-element.29.here, f32[64,128]{1,0:T(8,128)S(1)} %collective-permute-done.19.there), custom_call_target="tpu_custom_call" | custom-call | flops 65536 | bytes 262144 | tf_op jit(solution)/shard_map/gram/pallas_call | solution.py:193
  39.7 0.6 %collective-permute-done.16 = f32[8,128]{1,0:T(8,128)S(1)} collective-permute-done((f32[8,128]{1,0:T(8,128)S(1)}, f32[8,128]{1,0:T(8,128)S(1)}, u32[]{:S(2)}, u32[]{:S(2)}) %collective-permute-start.16) | collective-permute-done | bytes 4128 | tf_op jit(solution)/shard_map/gram/ppermute | solution.py:225
  40.2 0.0 collective-permute-done.17
  40.2 0.0 collective-permute-done.18
  40.2 0.6 %slice.27 = f32[2,16]{1,0:T(2,128)} slice(f32[8,128]{1,0:T(8,128)S(1)} %add_select_fusion), slice={[0:2], [0:16]} | slice | bytes 256 | tf_op jit(solution)/shard_map/gram/slice | solution.py:273
  (9 shorter events, 0.1 us)
Async XLA Ops:
  8.8 2.5 %collective-permute-start = (f32[256,128]{1,0:T(8,128)S(1)}, f32[256,128]{1,0:T(8,128)S(1)}, u32[]{:S(2)}, u32[]{:S(2)}) collective-permute-start(f32[256,128]{1,0:T(8,128)S(1)} %slice.29), channel_id=1, source_target_pairs={{0,1},{1,0},{2,3},{3,2},{4,5},{5,4},{6,7},{7,6},{8,9},{9,8},{10,11... | collective-permute-start | bytes 393224 | tf_op jit(solution)/shard_map/reduce/ppermute | solution.py:212
  11.3 4.7 %collective-permute-start.1 = (f32[256,128]{1,0:T(8,128)S(1)}, f32[256,128]{1,0:T(8,128)S(1)}, u32[]{:S(2)}, u32[]{:S(2)}) collective-permute-start(f32[256,128]{1,0:T(8,128)S(1)} %slice_add_fusion), channel_id=1, source_target_pairs={{0,3},{1,0},{2,1},{3,2},{4,7},{5,4},{6,5},{7,6},{8,11},{9,8},{10,9... | collective-permute-start | bytes 393224 | tf_op jit(solution)/shard_map/reduce/ppermute | solution.py:220
  16.0 4.0 %collective-permute-start.2 = (f32[64,128]{1,0:T(8,128)S(1)}, f32[64,128]{1,0:T(8,128)S(1)}, u32[]{:S(2)}, u32[]{:S(2)}) collective-permute-start(f32[64,128]{1,0:T(8,128)S(1)} %get-tuple-element.37), channel_id=1, source_target_pairs={{1,8},{0,1},{3,10},{2,3},{5,12},{4,5},{7,14},{6,7},{9,0},{8,9},{11... | collective-permute-start | bytes 98312 | tf_op jit(solution)/shard_map/reduce/ppermute | solution.py:220
  18.7 1.3 %collective-permute-start.3 = (f32[64,128]{1,0:T(8,128)S(1)}, f32[64,128]{1,0:T(8,128)S(1)}, u32[]{:S(2)}, u32[]{:S(2)}) collective-permute-start(f32[64,128]{1,0:T(8,128)S(1)} %get-tuple-element.36), channel_id=1, source_target_pairs={{1,4},{0,1},{3,6},{2,3},{5,8},{4,5},{7,10},{6,7},{9,12},{8,9},{11,... | collective-permute-start | bytes 98312 | tf_op jit(solution)/shard_map/reduce/ppermute | solution.py:220
  18.7 2.3 %collective-permute-start.4 = (f32[64,128]{1,0:T(8,128)S(1)}, f32[64,128]{1,0:T(8,128)S(1)}, u32[]{:S(2)}, u32[]{:S(2)}) collective-permute-start(f32[64,128]{1,0:T(8,128)S(1)} %get-tuple-element.35), channel_id=1, source_target_pairs={{1,12},{0,1},{3,14},{2,3},{5,0},{4,5},{7,2},{6,7},{9,4},{8,9},{11,... | collective-permute-start | bytes 98312 | tf_op jit(solution)/shard_map/reduce/ppermute | solution.py:220
  20.0 1.2 %collective-permute-start.5 = (f32[64,128]{1,0:T(8,128)S(1)}, f32[64,128]{1,0:T(8,128)S(1)}, u32[]{:S(2)}, u32[]{:S(2)}) collective-permute-start(f32[64,128]{1,0:T(8,128)S(1)} %get-tuple-element.34), channel_id=1, source_target_pairs={{0,1},{1,0},{2,3},{3,2},{4,5},{5,4},{6,7},{7,6},{8,9},{9,8},{10,11... | collective-permute-start | bytes 98312 | tf_op jit(solution)/shard_map/reduce/ppermute | solution.py:212
  21.2 5.2 %collective-permute-start.6 = (f32[64,128]{1,0:T(8,128)S(1)}, f32[64,128]{1,0:T(8,128)S(1)}, u32[]{:S(2)}, u32[]{:S(2)}) collective-permute-start(f32[64,128]{1,0:T(8,128)S(1)} %add_add_fusion), channel_id=1, source_target_pairs={{0,19},{1,0},{2,17},{3,2},{4,23},{5,4},{6,21},{7,6},{8,27},{9,8},{... | collective-permute-start | bytes 98312 | tf_op jit(solution)/shard_map/gather/ppermute | solution.py:220
  22.7 3.7 %collective-permute-start.7 = (f32[64,128]{1,0:T(8,128)S(1)}, f32[64,128]{1,0:T(8,128)S(1)}, u32[]{:S(2)}, u32[]{:S(2)}) collective-permute-start(f32[64,128]{1,0:T(8,128)S(1)} %add_add_fusion), channel_id=1, source_target_pairs={{0,1},{1,0},{2,3},{3,2},{4,5},{5,4},{6,7},{7,6},{8,9},{9,8},{10,11... | collective-permute-start | bytes 98312 | tf_op jit(solution)/shard_map/gather/ppermute | solution.py:212
  26.4 3.7 %collective-permute-start.10 = (f32[128,128]{1,0:T(8,128)S(1)}, f32[128,128]{1,0:T(8,128)S(1)}, u32[]{:S(2)}, u32[]{:S(2)}) collective-permute-start(f32[128,128]{1,0:T(8,128)S(1)} %get-tuple-element.39), channel_id=1, source_target_pairs={{1,64},{0,1},{3,66},{2,3},{5,68},{4,5},{7,70},{6,7},{9,72},{8,9},{... | collective-permute-start | bytes 196616 | tf_op jit(solution)/shard_map/gather/ppermute | solution.py:220
  28.8 1.9 %collective-permute-start.11 = (f32[128,128]{1,0:T(8,128)S(1)}, f32[128,128]{1,0:T(8,128)S(1)}, u32[]{:S(2)}, u32[]{:S(2)}) collective-permute-start(f32[128,128]{1,0:T(8,128)S(1)} %get-tuple-element.39), channel_id=1, source_target_pairs={{1,32},{0,1},{3,34},{2,3},{5,36},{4,5},{7,38},{6,7},{9,40},{8,9},{... | collective-permute-start | bytes 196616 | tf_op jit(solution)/shard_map/gather/ppermute | solution.py:220
  28.8 2.5 %collective-permute-start.8 = (f32[128,128]{1,0:T(8,128)S(1)}, f32[128,128]{1,0:T(8,128)S(1)}, u32[]{:S(2)}, u32[]{:S(2)}) collective-permute-start(f32[128,128]{1,0:T(8,128)S(1)} %get-tuple-element.39), channel_id=1, source_target_pairs={{1,96},{0,1},{3,98},{2,3},{5,100},{4,5},{7,102},{6,7},{9,104},{8,9... | collective-permute-start | bytes 196616 | tf_op jit(solution)/shard_map/gather/ppermute | solution.py:220
  29.9 1.3 %collective-permute-start.9 = (f32[128,128]{1,0:T(8,128)S(1)}, f32[128,128]{1,0:T(8,128)S(1)}, u32[]{:S(2)}, u32[]{:S(2)}) collective-permute-start(f32[128,128]{1,0:T(8,128)S(1)} %get-tuple-element.39), channel_id=1, source_target_pairs={{0,1},{1,0},{2,3},{3,2},{4,5},{5,4},{6,7},{7,6},{8,9},{9,8},{10,11... | collective-permute-start | bytes 196616 | tf_op jit(solution)/shard_map/gather/ppermute | solution.py:212
  31.5 4.6 %collective-permute-start.12 = (f32[8,128]{1,0:T(8,128)S(1)}, f32[8,128]{1,0:T(8,128)S(1)}, u32[]{:S(2)}, u32[]{:S(2)}) collective-permute-start(f32[8,128]{1,0:T(8,128)S(1)} %gram.2), channel_id=1, source_target_pairs={{0,9},{1,0},{2,11},{3,2},{4,13},{5,4},{6,15},{7,6},{8,1},{9,8},{10... | collective-permute-start | bytes 12296 | tf_op jit(solution)/shard_map/gram/ppermute | solution.py:220
  33.3 4.2 %collective-permute-start.13 = (f32[8,128]{1,0:T(8,128)S(1)}, f32[8,128]{1,0:T(8,128)S(1)}, u32[]{:S(2)}, u32[]{:S(2)}) collective-permute-start(f32[8,128]{1,0:T(8,128)S(1)} %gram.2), channel_id=1, source_target_pairs={{0,5},{1,0},{2,7},{3,2},{4,9},{5,4},{6,11},{7,6},{8,13},{9,8},{10,... | collective-permute-start | bytes 12296 | tf_op jit(solution)/shard_map/gram/ppermute | solution.py:220
  33.4 4.2 %collective-permute-start.14 = (f32[8,128]{1,0:T(8,128)S(1)}, f32[8,128]{1,0:T(8,128)S(1)}, u32[]{:S(2)}, u32[]{:S(2)}) collective-permute-start(f32[8,128]{1,0:T(8,128)S(1)} %gram.2), channel_id=1, source_target_pairs={{0,13},{1,0},{2,15},{3,2},{4,1},{5,4},{6,3},{7,6},{8,5},{9,8},{10,... | collective-permute-start | bytes 12296 | tf_op jit(solution)/shard_map/gram/ppermute | solution.py:220
  33.9 3.6 %collective-permute-start.15 = (f32[8,128]{1,0:T(8,128)S(1)}, f32[8,128]{1,0:T(8,128)S(1)}, u32[]{:S(2)}, u32[]{:S(2)}) collective-permute-start(f32[8,128]{1,0:T(8,128)S(1)} %gram.2), channel_id=1, source_target_pairs={{0,1},{1,0},{2,3},{3,2},{4,5},{5,4},{6,7},{7,6},{8,9},{9,8},{10,11... | collective-permute-start | bytes 12296 | tf_op jit(solution)/shard_map/gram/ppermute | solution.py:212
  35.7 3.0 %collective-permute-start.19 = (f32[64,128]{1,0:T(8,128)S(1)}, f32[64,128]{1,0:T(8,128)S(1)}, u32[]{:S(2)}, u32[]{:S(2)}) collective-permute-start(f32[64,128]{1,0:T(8,128)S(1)} %get-tuple-element.29.here), channel_id=1, source_target_pairs={{0,2},{1,3},{2,0},{3,1},{4,6},{5,7},{6,4},{7,5},{8,10},{9,11},{10,... | collective-permute-start | bytes 98312 | tf_op jit(solution)/shard_map/gram/ppermute | solution.py:225
  37.5 2.7 %collective-permute-start.16 = (f32[8,128]{1,0:T(8,128)S(1)}, f32[8,128]{1,0:T(8,128)S(1)}, u32[]{:S(2)}, u32[]{:S(2)}) collective-permute-start(f32[8,128]{1,0:T(8,128)S(1)} %add_add_fusion.1), channel_id=1, source_target_pairs={{0,2},{1,3},{2,0},{3,1},{4,6},{5,7},{6,4},{7,5},{8,10},{9,11},{10,... | collective-permute-start | bytes 12296 | tf_op jit(solution)/shard_map/gram/ppermute | solution.py:225
  38.0 2.3 %collective-permute-start.17 = (f32[8,128]{1,0:T(8,128)S(1)}, f32[8,128]{1,0:T(8,128)S(1)}, u32[]{:S(2)}, u32[]{:S(2)}) collective-permute-start(f32[8,128]{1,0:T(8,128)S(1)} %add_add_fusion.1), channel_id=1, source_target_pairs={{1,2},{0,1},{3,0},{2,3},{5,6},{4,5},{7,4},{6,7},{9,10},{8,9},{11,8... | collective-permute-start | bytes 12296 | tf_op jit(solution)/shard_map/gram/ppermute | solution.py:220
  38.6 1.6 %collective-permute-start.18 = (f32[8,128]{1,0:T(8,128)S(1)}, f32[8,128]{1,0:T(8,128)S(1)}, u32[]{:S(2)}, u32[]{:S(2)}) collective-permute-start(f32[8,128]{1,0:T(8,128)S(1)} %add_add_fusion.1), channel_id=1, source_target_pairs={{0,1},{1,0},{2,3},{3,2},{4,5},{5,4},{6,7},{7,6},{8,9},{9,8},{10,11... | collective-permute-start | bytes 12296 | tf_op jit(solution)/shard_map/gram/ppermute | solution.py:212
where the time goes:
time: 40.9 us; the launch traced here: 40.8 us
  starting transfers between devices  18.2 us (44%)
  waiting for transfers between devices  11.9 us (29%)
  Pallas kernels  9.38 us (23%)
  between operations  0.69 us (2%)
  local copies, waits for them, and re-layouts  0.59 us (1%)
    ppermute x12, starting transfers between devices, send(): return lax.ppermute(v, AXES, pairs)  12.5 us
    ppermute x12, waiting for transfers between devices, send(): return lax.ppermute(v, AXES, pairs)  10.2 us
    pallas_call x1, Pallas kernels, project(): pl.pallas_call(project_kernel, out_shape=pltpu.VMEM((512, 128), F32), in_...  8.14 us
    ppermute x6, starting transfers between devices, swap(): return lax.ppermute(v, AXES, pairs)  4.93 us
    ppermute x6, waiting for transfers between devices, swap(): return lax.ppermute(v, AXES, pairs)  1.18 us
    pallas_call x1, Pallas kernels, arrange(): pl.pallas_call(arrange_kernel, out_shape=jax.ShapeDtypeStruct((16, 2, 8,...  1.01 us
  transfers between devices with their start and end apart: 20, of which 12 were waited for; matrix products, arithmetic and copies ran while one was open for 0% of the time, Pallas kernels for 2%

commit v1 on v0

--- a/solution.py
+++ b/solution.py
@@ -10,7 +10,6 @@
 BF16 = jnp.bfloat16
 AXES = ("gx", "gy", "gz")
 ROWS = 64
-REGION = 64
 
 
 def split(v):
@@ -28,17 +27,60 @@
     return jnp.where(f(i, j), 1.0, 0.0).astype(F32)
 
 
-def project_kernel(
-    field, second_hbm, third_hbm, species_hbm, out, window, spread, v_both, high, low,
-    second, third, species, sems, factor_sems,
+def species_step(k, piece, spread, high, low):
+    count, _, columns = piece.shape
+    w_both = spread[...]
+    for g in range(ROWS // 16):
+        parts = []
+        for at in (g * 16, g * 16 + 8):
+            f_high, f_low = split(piece[:, at : at + 8, :].reshape(count * 8, columns))
+            d = dot(w_both, f_high)
+            d = d[:64] + d[64:] + dot(w_both[:64], f_low)
+            parts.append(d.reshape(8, 8, columns))
+        r_high, r_low = split(jnp.concatenate(parts, axis=1))
+        at = pl.ds(pl.multiple_of(k * ROWS + g * 16, 16), 16)
+        high[:, at, :] = r_high
+        low[:, at, :] = r_low
+
+
+def modes(out, high, low, u_both, v_both, last_high=None, last_low=None):
+    ts = []
+    for r in range(8):
+        r_high, r_low = high[r], low[r]
+        if last_high is not None:
+            r_high = jnp.concatenate([r_high[: -ROWS], last_high[r]], axis=0)
+            r_low = jnp.concatenate([r_low[: -ROWS], last_low[r]], axis=0)
+        d = dot(u_both[...], r_high)
+        ts.append(d[:64] + d[64:] + dot(u_both[0:64], r_low))
+    t_high, t_low = split(jnp.concatenate(ts, axis=0))
+    e = dot(jnp.concatenate([t_high, t_low], axis=0), v_both[0])
+    e = (e[:512] + e[512:] + dot(t_high, v_both[1])).reshape(8, 64, 256)
+    lane = lax.broadcasted_iota(jnp.int32, (64, 256), 1) % 128 // 32
+    for half in range(2):
+        total = e[half * 4]
+        for q in range(1, 4):
+            total = jnp.where(lane == q, e[half * 4 + q], total)
+        for zs in range(2):
+            for xs in range(4):
+                at = zs * 128 + xs * 32 + half * 16
+                out[at : at + 16, :] = total[xs * 16 : xs * 16 + 16, zs * 128 : zs * 128 + 128]
+
+
+def first_kernel(
+    field, second_hbm, third_hbm, species_hbm, out, later, next_high, next_low, spread, u_both, v_both,
+    window, high, low, second, third, species, sems, factor_sems,
 ):
     planes, count, rows, columns = field.shape
     per = rows // ROWS
 
-    def copy(c):
-        p, k = c // per, c % per
+    last = planes * per - 1
+
+    def copy(c, target=None):
+        rows_at = pl.ds(pl.multiple_of(c % per * ROWS, ROWS), ROWS)
         return pltpu.make_async_copy(
-            field.at[p, :, pl.ds(k * ROWS, ROWS), :], window.at[c], sems.at[c]
+            field.at[c // per, :, rows_at, :],
+            window.at[c] if target is None else target,
+            sems.at[c],
         )
 
     factors = [
@@ -53,99 +95,95 @@
         copy(c).start()
     for factor in factors:
         factor.wait()
-    for c in range(2, planes * per):
+    for c in range(2, last):
         copy(c).start()
+    copy(last, later).start()
     x = lax.axis_index("gy")
     given = lax.axis_index("gz") // 2 ^ lax.axis_index("gz") % 2 ^ lax.axis_index("gx") % 2
 
     r_of = mask((64, 8), lambda i, j: i // 8 == j)
     s_of = mask((32, 256), lambda i, j: j // 8 == i)
     w = jnp.dot(jnp.dot(r_of, species[...], precision=HIGHEST), s_of, precision=HIGHEST)
-    w_high, w_low = split(w * mask((64, 256), lambda i, j: i % 8 == j % 8))
-    spread[0:64] = w_high
-    spread[64:128] = w_low
+    spread[0:64], spread[64:128] = split(w * mask((64, 256), lambda i, j: i % 8 == j % 8))
 
     def rank_second(i):
         return (x + i // 16) % 4 * 16 + i % 16
 
     u = jnp.dot(mask((64, 64), lambda i, j: rank_second(i) == j), second[...], precision=HIGHEST)
-    u_high, u_low = split(u)
-    u_both = jnp.concatenate([u_high, u_low], axis=0)
+    u_both[0:64], u_both[64:128] = split(u)
 
     pick = mask((256, 64), lambda i, j: j == (given ^ i // 128) * 32 + i % 32)
     v = lax.dot_general(third[...], pick, (((0,), (1,)), ((), ())), precision=HIGHEST)
     v_both[0], v_both[1] = split(v)
-    lane = lax.broadcasted_iota(jnp.int32, (64, 256), 1) % 128 // 32
-
-    for p in range(planes):
-
-        def step(k, carry, p=p):
-            first = p * per + k * (REGION // ROWS)
-            for c in range(REGION // ROWS):
-                copy(first + c).wait()
-            w_both = spread[...]
-            for g in range(REGION // 16):
-                parts = []
-                for h in range(2):
-                    at = g * 16 + h * 8
-                    f = window[first + at // ROWS, :, at % ROWS : at % ROWS + 8, :]
-                    f_high, f_low = split(f.reshape(count * 8, columns))
-                    d = dot(w_both, f_high)
-                    d = d[:64] + d[64:] + dot(w_both[:64], f_low)
-                    parts.append(d.reshape(8, 8, columns))
-                r_high, r_low = split(jnp.concatenate(parts, axis=1))
-                at = pl.ds(pl.multiple_of(k * REGION + g * 16, 16), 16)
-                high[:, at, :] = r_high
-                low[:, at, :] = r_low
-            return carry
-
-        lax.fori_loop(0, rows // REGION, step, 0)
-        ts = []
-        for r in range(8):
-            d = dot(u_both, high[r])
-            ts.append(d[:64] + d[64:] + dot(u_both[:64], low[r]))
-        t_high, t_low = split(jnp.concatenate(ts, axis=0))
-        e = dot(jnp.concatenate([t_high, t_low], axis=0), v_both[0])
-        e = (e[:512] + e[512:] + dot(t_high, v_both[1])).reshape(8, 64, 256)
-        for half in range(2):
-            total = e[half * 4]
-            for q in range(1, 4):
-                total = jnp.where(lane == q, e[half * 4 + q], total)
-            for zs in range(2):
-                for xs in range(4):
-                    at = zs * 256 + xs * 64 + p * 32 + half * 16
-                    out[at : at + 16, :] = total[xs * 16 : xs * 16 + 16, zs * 128 : zs * 128 + 128]
+
+    def step(k, carry):
+        copy(k).wait()
+        species_step(k, window.at[k], spread, high, low)
+        return carry
+
+    def next_step(k, carry):
+        copy(per + k).wait()
+        species_step(k, window.at[per + k], spread, next_high, next_low)
+        return carry
+
+    lax.fori_loop(0, per, step, 0)
+    modes(out, high, low, u_both, v_both)
+    lax.fori_loop(0, per - 1, next_step, 0)
+    copy(last, later).wait()
+
+
+def second_kernel(later, next_high, next_low, spread, u_both, v_both, out, high, low):
+    species_step(0, later, spread, high, low)
+    modes(out, next_high, next_low, u_both, v_both, high, low)
 
 
 def project(field, second, third, species):
     planes, count, rows, columns = field.shape
     vmem = pl.BlockSpec(memory_space=pltpu.VMEM)
-    pieces = planes * rows // ROWS
-    return pl.pallas_call(
-        project_kernel,
-        out_shape=pltpu.VMEM((512, 128), F32),
-        in_specs=[pl.BlockSpec(memory_space=pltpu.HBM)] * 4,
-        out_specs=vmem,
-        scratch_shapes=[
-            pltpu.VMEM((pieces, count, ROWS, columns), F32),
+    per = rows // ROWS
+    one, *kept = pl.pallas_call(
+        first_kernel,
+        out_shape=[
+            pltpu.VMEM((256, 128), F32),
+            pltpu.VMEM((count, ROWS, columns), F32),
+            pltpu.VMEM((8, rows, columns), BF16),
+            pltpu.VMEM((8, rows, columns), BF16),
+            pltpu.VMEM((128, 256), BF16),
             pltpu.VMEM((128, 256), BF16),
             pltpu.VMEM((2, columns, 256), BF16),
+        ],
+        in_specs=[pl.BlockSpec(memory_space=pltpu.HBM)] * 4,
+        out_specs=[vmem] * 7,
+        scratch_shapes=[
+            pltpu.VMEM((planes * per - 1, count, ROWS, columns), F32),
             pltpu.VMEM((8, rows, columns), BF16),
             pltpu.VMEM((8, rows, columns), BF16),
             pltpu.VMEM(second.shape, F32),
             pltpu.VMEM(third.shape, F32),
             pltpu.VMEM(species.shape, F32),
-            pltpu.SemaphoreType.DMA((pieces,)),
+            pltpu.SemaphoreType.DMA((planes * per,)),
             pltpu.SemaphoreType.DMA((3,)),
         ],
-        compiler_params=pltpu.CompilerParams(vmem_limit_bytes=48 << 20),
+        compiler_params=pltpu.CompilerParams(vmem_limit_bytes=32 << 20),
         cost_estimate=pl.CostEstimate(
-            flops=1 << 32, bytes_accessed=17 << 20, transcendentals=0
+            flops=1 << 31, bytes_accessed=17 << 20, transcendentals=0
         ),
-    )(field, *[pltpu.with_memory_space_constraint(v, pltpu.HBM) for v in (second, third, species)])
-
-
-def gram_kernel(three, mine, two, one, out):
+    )(*[pltpu.with_memory_space_constraint(v, pltpu.HBM) for v in (field, second, third, species)])
+    two = pl.pallas_call(
+        second_kernel,
+        out_shape=pltpu.VMEM((256, 128), F32),
+        in_specs=[vmem] * 6,
+        out_specs=vmem,
+        scratch_shapes=[pltpu.VMEM((8, ROWS, columns), BF16)] * 2,
+        compiler_params=pltpu.CompilerParams(vmem_limit_bytes=16 << 20),
+        cost_estimate=pl.CostEstimate(
+            flops=1 << 31, bytes_accessed=9 << 20, transcendentals=0
+        ),
+    )(*[pltpu.with_memory_space_constraint(v, pltpu.VMEM) for v in kept])
+    return one, two
+
+
+def gram_kernel(two, one, three, mine, out):
     gx = lax.axis_index("gx")
     y, h = gx // 2, gx % 2
     sums = []
@@ -246,13 +284,18 @@
 
 
 def on_device(field_window, second_factor, third_factor, species_factor):
-    part = project(field_window, second_factor.T, third_factor.T, species_factor.T)
+    one, two = project(field_window, second_factor.T, third_factor.T, species_factor.T)
     first_core = lax.axis_index("gz") % 2 == 0
     with jax.named_scope("reduce"):
-        part = part[256:] + swap(part[:256])
-        part = send(part, 0, over_z) + part
-        terms = [send(part[64 * k : 64 * k + 64], 1, over_x(k)) for k in (2, 1, 3)]
-        terms = together(*terms, swap(part[:64]))
+        given = swap(one[:128])
+        two, given = together(two, given)
+        one = one[128:] + given
+        far = send(one, 0, over_z)
+        two = two[128:] + swap(two[:128])
+        parts = [far + one, send(two, 0, over_z) + two]
+        pieces = [jnp.concatenate([part[32 * k : 32 * k + 32] for part in parts]) for k in range(4)]
+        terms = [swap(pieces[0]), *[send(pieces[k], 1, over_x(k)) for k in (3, 1, 2)]]
+        terms = together(*terms)
         block = ((terms[0] + terms[1]) + terms[2]) + terms[3]
     with jax.named_scope("gather"):
         far, mine = together(send(block, 0, over_h), swap(block))
@@ -260,7 +303,7 @@
         two, one, three = [send(near, 1, over_y(k)) for k in (2, 1, 3)]
         near = swap(near)
     with jax.named_scope("gram"):
-        total = gram(three, near, two, one)
+        total = gram(two, one, three, near)
         total, here = together(total, jnp.where(first_core, block, mine))
         there = trade(here)
         terms = [send(total, 0, over_x(k)) for k in (2, 1, 3)]

time: 40.9 us -> 40.7 us (level)
  waiting for transfers between devices: 11.9 us -> 10.1 us
  starting transfers between devices: 18.2 us -> 19.7 us
    ppermute x12 -> x13, waiting for transfers between devices: 10.2 us -> 8.65 us  [send(): return lax.ppermute(v, AXES, pairs)]
    ppermute x12 -> x13, starting transfers between devices: 12.5 us -> 13.8 us  [send(): return lax.ppermute(v, AXES, pairs)]
    ppermute x6 -> x7, waiting for transfers between devices: 1.18 us -> 0.86 us  [swap(): return lax.ppermute(v, AXES, pairs)]
    pallas_call x1 -> x2, Pallas kernels: 8.14 us -> 8.2 us  [the longest x1 6.9 us: project(): pl.pallas_call(first_kernel, out_shape=[pltpu.VMEM((256, 128), F32), pltp...]
    ppermute x6 -> x7, starting transfers between devices: 4.93 us -> 4.92 us  [swap(): return lax.ppermute(v, AXES, pairs)]
  transfers between devices with their start and end apart: 20 -> 22, of which waited for: 12 -> 12; matrix products, arithmetic and copies ran while one was open for 0% -> 0% of each run, Pallas kernels for 2% -> 6%
where the time goes in v1:
time: 40.7 us; the launch traced here: 40.6 us
  starting transfers between devices  19.7 us (48%)
  waiting for transfers between devices  10.1 us (25%)
  Pallas kernels  9.44 us (23%)
  between operations  0.75 us (2%)
  local copies, waits for them, and re-layouts  0.6 us (1%)
    ppermute x13, starting transfers between devices, send(): return lax.ppermute(v, AXES, pairs)  13.8 us
    ppermute x13, waiting for transfers between devices, send(): return lax.ppermute(v, AXES, pairs)  8.65 us
    pallas_call x1, Pallas kernels, project(): pl.pallas_call(first_kernel, out_shape=[pltpu.VMEM((256, 128), F32), pltp...  6.9 us
    ppermute x7, starting transfers between devices, swap(): return lax.ppermute(v, AXES, pairs)  4.92 us
    pallas_call x1, Pallas kernels, project(): pl.pallas_call(second_kernel, out_shape=pltpu.VMEM((256, 128), F32), in_s...  1.3 us
    pallas_call x1, Pallas kernels, arrange(): pl.pallas_call(arrange_kernel, out_shape=jax.ShapeDtypeStruct((16, 2, 8,...  1.01 us
    ppermute x2, starting transfers between devices, trade(): return lax.ppermute(v, AXES, pairs)  0.9 us
    ppermute x7, waiting for transfers between devices, swap(): return lax.ppermute(v, AXES, pairs)  0.86 us
  transfers between devices with their start and end apart: 22, of which 12 were waited for; matrix products, arithmetic and copies ran while one was open for 0% of the time, Pallas kernels for 6%

profile of v1, /device:TPU:1, one launch (start us, length us, event | category | flops | bytes accessed | tf_op | source)
XLA Modules:
  0.0 40.6 jit_solution(6999898844520190435)
XLA Ops:
  0.6 6.9 %shard_map.59 = (f32[256,128]{1,0:T(8,128)S(1)}, f32[32,64,256]{2,1,0:T(8,128)S(1)}, bf16[8,256,256]{2,1,0:T(8,128)(2,1)S(1)}, bf16[8,256,256]{2,1,0:T(8,128)(2,...) custom-call(f32[2,32,256,256]{3,2,1,0:T(8,128)} %field.1, ...), custom_call_target="tpu_custom_call" | custom-call | flops 2147483648 | bytes 17825792 | tf_op jit(solution)/shard_map/pallas_call | solution.py:144
  7.6 1.5 %collective-permute-start = (f32[128,128]{1,0:T(8,128)S(1)}, f32[128,128]{1,0:T(8,128)S(1)}, u32[]{:S(2)}, u32[]{:S(2)}) collective-permute-start(f32[128,128]{1,0:T(8,128)S(1)} %slice.40), channel_id=1, source_target_pairs={{0,1},{1,0},{2,3},{3,2},{4,5},{5,4},{6,7},{7,6},{8,9},{9,8},{10,11... | collective-permute-start | bytes 196616 | tf_op jit(solution)/shard_map/reduce/ppermute | solution.py:250
  9.1 1.3 %shard_map.60 = f32[256,128]{1,0:T(8,128)S(1)} custom-call(f32[32,64,256]{2,1,0:T(8,128)S(1)} %get-tuple-element.28.later, bf16[8,256,256]{2,1,0:T(8,128)(2,1)S(1)} %get-tuple-element.29.next_high, bf16[8,256,256]{2,1,0:T(8,128)(2,1)S(1)} %get-tuple-element.30.next_low, bf16[128,256]{1,0:T(8,128)(2,1)S(1)} %get-tuple-element.31.spread, ...), custom_call_target="tpu_custom_call" | custom-call | flops 2147483648 | bytes 9437184 | tf_op jit(solution)/shard_map/pallas_call | solution.py:172
  10.4 0.0 collective-permute-done
  10.4 0.1 collective-permute-start.2
  10.5 0.6 %collective-permute-start.1 = (f32[128,128]{1,0:T(8,128)S(1)}, f32[128,128]{1,0:T(8,128)S(1)}, u32[]{:S(2)}, u32[]{:S(2)}) collective-permute-start(f32[128,128]{1,0:T(8,128)S(1)} %slice_add_fusion.1), channel_id=1, source_target_pairs={{0,3},{1,0},{2,1},{3,2},{4,7},{5,4},{6,5},{7,6},{8,11},{9,8},{10,9... | collective-permute-start | bytes 196616 | tf_op jit(solution)/shard_map/reduce/ppermute | solution.py:258
  11.1 0.7 %collective-permute-done.2 = f32[128,128]{1,0:T(8,128)S(1)} collective-permute-done((f32[128,128]{1,0:T(8,128)S(1)}, f32[128,128]{1,0:T(8,128)S(1)}, u32[]{:S(2)}, u32[]{:S(2)}) %collective-permute-start.2) | collective-permute-done | bytes 65568 | tf_op jit(solution)/shard_map/reduce/ppermute | solution.py:250
  11.7 1.0 %collective-permute-start.3 = (f32[128,128]{1,0:T(8,128)S(1)}, f32[128,128]{1,0:T(8,128)S(1)}, u32[]{:S(2)}, u32[]{:S(2)}) collective-permute-start(f32[128,128]{1,0:T(8,128)S(1)} %slice_add_fusion), channel_id=1, source_target_pairs={{0,3},{1,0},{2,1},{3,2},{4,7},{5,4},{6,5},{7,6},{8,11},{9,8},{10,9... | collective-permute-start | bytes 196616 | tf_op jit(solution)/shard_map/reduce/ppermute | solution.py:258
  12.8 1.8 %collective-permute-done.1 = f32[128,128]{1,0:T(8,128)S(1)} collective-permute-done((f32[128,128]{1,0:T(8,128)S(1)}, f32[128,128]{1,0:T(8,128)S(1)}, u32[]{:S(2)}, u32[]{:S(2)}) %collective-permute-start.1) | collective-permute-done | bytes 65568 | tf_op jit(solution)/shard_map/reduce/ppermute | solution.py:258
  14.6 0.9 %collective-permute-done.3 = f32[128,128]{1,0:T(8,128)S(1)} collective-permute-done((f32[128,128]{1,0:T(8,128)S(1)}, f32[128,128]{1,0:T(8,128)S(1)}, u32[]{:S(2)}, u32[]{:S(2)}) %collective-permute-start.3) | collective-permute-done | bytes 65568 | tf_op jit(solution)/shard_map/reduce/ppermute | solution.py:258
  15.6 3.0 %collective-permute-start.7 = (f32[64,128]{1,0:T(8,128)S(1)}, f32[64,128]{1,0:T(8,128)S(1)}, u32[]{:S(2)}, u32[]{:S(2)}) collective-permute-start(f32[64,128]{1,0:T(8,128)S(1)} %pad_maximum_fusion.3), channel_id=1, source_target_pairs={{1,8},{0,1},{3,10},{2,3},{5,12},{4,5},{7,14},{6,7},{9,0},{8,9},{11... | collective-permute-start | bytes 98312 | tf_op jit(solution)/shard_map/reduce/ppermute | solution.py:258
  18.6 0.0 collective-permute-start.6
  18.6 1.3 %collective-permute-start.5 = (f32[64,128]{1,0:T(8,128)S(1)}, f32[64,128]{1,0:T(8,128)S(1)}, u32[]{:S(2)}, u32[]{:S(2)}) collective-permute-start(f32[64,128]{1,0:T(8,128)S(1)} %pad_maximum_fusion.1), channel_id=1, source_target_pairs={{1,12},{0,1},{3,14},{2,3},{5,0},{4,5},{7,2},{6,7},{9,4},{8,9},{11,... | collective-permute-start | bytes 98312 | tf_op jit(solution)/shard_map/reduce/ppermute | solution.py:258
  19.8 0.0 collective-permute-start.4
  19.8 0.0 collective-permute-done.7
  19.8 0.1 collective-permute-done.6
  19.9 1.0 %collective-permute-done.5 = f32[64,128]{1,0:T(8,128)S(1)} collective-permute-done((f32[64,128]{1,0:T(8,128)S(1)}, f32[64,128]{1,0:T(8,128)S(1)}, u32[]{:S(2)}, u32[]{:S(2)}) %collective-permute-start.5) | collective-permute-done | bytes 32800 | tf_op jit(solution)/shard_map/reduce/ppermute | solution.py:258
  20.9 0.2 collective-permute-done.4
  21.1 1.5 %collective-permute-start.8 = (f32[64,128]{1,0:T(8,128)S(1)}, f32[64,128]{1,0:T(8,128)S(1)}, u32[]{:S(2)}, u32[]{:S(2)}) collective-permute-start(f32[64,128]{1,0:T(8,128)S(1)} %add_add_fusion), channel_id=1, source_target_pairs={{0,19},{1,0},{2,17},{3,2},{4,23},{5,4},{6,21},{7,6},{8,27},{9,8},{... | collective-permute-start | bytes 98312 | tf_op jit(solution)/shard_map/gather/ppermute | solution.py:258
  22.5 1.6 %collective-permute-start.9 = (f32[64,128]{1,0:T(8,128)S(1)}, f32[64,128]{1,0:T(8,128)S(1)}, u32[]{:S(2)}, u32[]{:S(2)}) collective-permute-start(f32[64,128]{1,0:T(8,128)S(1)} %add_add_fusion), channel_id=1, source_target_pairs={{0,1},{1,0},{2,3},{3,2},{4,5},{5,4},{6,7},{7,6},{8,9},{9,8},{10,11... | collective-permute-start | bytes 98312 | tf_op jit(solution)/shard_map/gather/ppermute | solution.py:250
  24.1 2.1 %collective-permute-done.8 = f32[64,128]{1,0:T(8,128)S(1)} collective-permute-done((f32[64,128]{1,0:T(8,128)S(1)}, f32[64,128]{1,0:T(8,128)S(1)}, u32[]{:S(2)}, u32[]{:S(2)}) %collective-permute-start.8) | collective-permute-done | bytes 32800 | tf_op jit(solution)/shard_map/gather/ppermute | solution.py:258
  26.2 0.0 collective-permute-done.9
  26.3 2.3 %collective-permute-start.10 = (f32[128,128]{1,0:T(8,128)S(1)}, f32[128,128]{1,0:T(8,128)S(1)}, u32[]{:S(2)}, u32[]{:S(2)}) collective-permute-start(f32[128,128]{1,0:T(8,128)S(1)} %get-tuple-element.61), channel_id=1, source_target_pairs={{1,64},{0,1},{3,66},{2,3},{5,68},{4,5},{7,70},{6,7},{9,72},{8,9},{... | collective-permute-start | bytes 196616 | tf_op jit(solution)/shard_map/gather/ppermute | solution.py:258
  28.6 0.0 collective-permute-start.11
  28.6 1.2 %collective-permute-start.12 = (f32[128,128]{1,0:T(8,128)S(1)}, f32[128,128]{1,0:T(8,128)S(1)}, u32[]{:S(2)}, u32[]{:S(2)}) collective-permute-start(f32[128,128]{1,0:T(8,128)S(1)} %get-tuple-element.61), channel_id=1, source_target_pairs={{1,96},{0,1},{3,98},{2,3},{5,100},{4,5},{7,102},{6,7},{9,104},{8,9... | collective-permute-start | bytes 196616 | tf_op jit(solution)/shard_map/gather/ppermute | solution.py:258
  29.7 0.0 collective-permute-start.13
  29.7 0.2 collective-permute-done.10.two
  29.9 0.6 %collective-permute-done.11.one = f32[128,128]{1,0:T(8,128)S(1)} collective-permute-done((f32[128,128]{1,0:T(8,128)S(1)}, f32[128,128]{1,0:T(8,128)S(1)}, u32[]{:S(2)}, u32[]{:S(2)}) %collective-permute-start.11) | collective-permute-done | bytes 65568 | tf_op jit(solution)/shard_map/gather/ppermute | solution.py:258
  30.5 0.6 %collective-permute-done.12.three = f32[128,128]{1,0:T(8,128)S(1)} collective-permute-done((f32[128,128]{1,0:T(8,128)S(1)}, f32[128,128]{1,0:T(8,128)S(1)}, u32[]{:S(2)}, u32[]{:S(2)}) %collective-permute-start.12) | collective-permute-done | bytes 65568 | tf_op jit(solution)/shard_map/gather/ppermute | solution.py:258
  31.1 0.0 collective-permute-done.13.mine
  31.1 0.2 gram.2
  31.3 1.8 %collective-permute-start.14 = (f32[8,128]{1,0:T(8,128)S(1)}, f32[8,128]{1,0:T(8,128)S(1)}, u32[]{:S(2)}, u32[]{:S(2)}) collective-permute-start(f32[8,128]{1,0:T(8,128)S(1)} %gram.2), channel_id=1, source_target_pairs={{0,9},{1,0},{2,11},{3,2},{4,13},{5,4},{6,15},{7,6},{8,1},{9,8},{10... | collective-permute-start | bytes 12296 | tf_op jit(solution)/shard_map/gram/ppermute | solution.py:258
  33.1 0.1 collective-permute-start.15
  33.2 0.6 %collective-permute-start.16 = (f32[8,128]{1,0:T(8,128)S(1)}, f32[8,128]{1,0:T(8,128)S(1)}, u32[]{:S(2)}, u32[]{:S(2)}) collective-permute-start(f32[8,128]{1,0:T(8,128)S(1)} %gram.2), channel_id=1, source_target_pairs={{0,13},{1,0},{2,15},{3,2},{4,1},{5,4},{6,3},{7,6},{8,5},{9,8},{10,... | collective-permute-start | bytes 12296 | tf_op jit(solution)/shard_map/gram/ppermute | solution.py:258
  33.7 1.7 %collective-permute-start.17 = (f32[8,128]{1,0:T(8,128)S(1)}, f32[8,128]{1,0:T(8,128)S(1)}, u32[]{:S(2)}, u32[]{:S(2)}) collective-permute-start(f32[8,128]{1,0:T(8,128)S(1)} %gram.2), channel_id=1, source_target_pairs={{0,1},{1,0},{2,3},{3,2},{4,5},{5,4},{6,7},{7,6},{8,9},{9,8},{10,11... | collective-permute-start | bytes 12296 | tf_op jit(solution)/shard_map/gram/ppermute | solution.py:250
  35.5 0.4 %collective-permute-start.21 = (f32[64,128]{1,0:T(8,128)S(1)}, f32[64,128]{1,0:T(8,128)S(1)}, u32[]{:S(2)}, u32[]{:S(2)}) collective-permute-start(f32[64,128]{1,0:T(8,128)S(1)} %get-tuple-element.47.here), channel_id=1, source_target_pairs={{0,2},{1,3},{2,0},{3,1},{4,6},{5,7},{6,4},{7,5},{8,10},{9,11},{10,... | collective-permute-start | bytes 98312 | tf_op jit(solution)/shard_map/gram/ppermute | solution.py:263
  35.9 0.0 collective-permute-done.14
  35.9 1.4 %collective-permute-done.15 = f32[8,128]{1,0:T(8,128)S(1)} collective-permute-done((f32[8,128]{1,0:T(8,128)S(1)}, f32[8,128]{1,0:T(8,128)S(1)}, u32[]{:S(2)}, u32[]{:S(2)}) %collective-permute-start.15) | collective-permute-done | bytes 4128 | tf_op jit(solution)/shard_map/gram/ppermute | solution.py:258
  37.3 0.0 collective-permute-done.16
  37.3 0.0 collective-permute-done.17
  37.3 0.5 %collective-permute-start.18 = (f32[8,128]{1,0:T(8,128)S(1)}, f32[8,128]{1,0:T(8,128)S(1)}, u32[]{:S(2)}, u32[]{:S(2)}) collective-permute-start(f32[8,128]{1,0:T(8,128)S(1)} %add_add_fusion.1), channel_id=1, source_target_pairs={{0,2},{1,3},{2,0},{3,1},{4,6},{5,7},{6,4},{7,5},{8,10},{9,11},{10,... | collective-permute-start | bytes 12296 | tf_op jit(solution)/shard_map/gram/ppermute | solution.py:263
  37.8 0.6 %collective-permute-start.19 = (f32[8,128]{1,0:T(8,128)S(1)}, f32[8,128]{1,0:T(8,128)S(1)}, u32[]{:S(2)}, u32[]{:S(2)}) collective-permute-start(f32[8,128]{1,0:T(8,128)S(1)} %add_add_fusion.1), channel_id=1, source_target_pairs={{1,2},{0,1},{3,0},{2,3},{5,6},{4,5},{7,4},{6,7},{9,10},{8,9},{11,8... | collective-permute-start | bytes 12296 | tf_op jit(solution)/shard_map/gram/ppermute | solution.py:258
  38.4 0.0 collective-permute-start.20
  38.4 0.0 collective-permute-done.21.there
  38.4 1.0 %gram.3 = f32[16,2,8,16]{3,2,1,0:T(8,128)} custom-call(f32[64,128]{1,0:T(8,128)S(1)} %get-tuple-element.47.here, f32[64,128]{1,0:T(8,128)S(1)} %collective-permute-done.21.there), custom_call_target="tpu_custom_call" | custom-call | flops 65536 | bytes 262144 | tf_op jit(solution)/shard_map/gram/pallas_call | solution.py:231
  39.5 0.6 %collective-permute-done.18 = f32[8,128]{1,0:T(8,128)S(1)} collective-permute-done((f32[8,128]{1,0:T(8,128)S(1)}, f32[8,128]{1,0:T(8,128)S(1)}, u32[]{:S(2)}, u32[]{:S(2)}) %collective-permute-start.18) | collective-permute-done | bytes 4128 | tf_op jit(solution)/shard_map/gram/ppermute | solution.py:263
  40.0 0.0 collective-permute-done.19
  40.0 0.0 collective-permute-done.20
  40.0 0.6 %slice.51 = f32[2,16]{1,0:T(2,128)} slice(f32[8,128]{1,0:T(8,128)S(1)} %add_select_fusion), slice={[0:2], [0:16]} | slice | bytes 256 | tf_op jit(solution)/shard_map/gram/slice | solution.py:316
  (17 shorter events, 0.1 us)
Async XLA Ops:
  7.6 2.8 %collective-permute-start = (f32[128,128]{1,0:T(8,128)S(1)}, f32[128,128]{1,0:T(8,128)S(1)}, u32[]{:S(2)}, u32[]{:S(2)}) collective-permute-start(f32[128,128]{1,0:T(8,128)S(1)} %slice.40), channel_id=1, source_target_pairs={{0,1},{1,0},{2,3},{3,2},{4,5},{5,4},{6,7},{7,6},{8,9},{9,8},{10,11... | collective-permute-start | bytes 196616 | tf_op jit(solution)/shard_map/reduce/ppermute | solution.py:250
  10.4 1.3 %collective-permute-start.2 = (f32[128,128]{1,0:T(8,128)S(1)}, f32[128,128]{1,0:T(8,128)S(1)}, u32[]{:S(2)}, u32[]{:S(2)}) collective-permute-start(f32[128,128]{1,0:T(8,128)S(1)} %slice.43), channel_id=1, source_target_pairs={{0,1},{1,0},{2,3},{3,2},{4,5},{5,4},{6,7},{7,6},{8,9},{9,8},{10,11... | collective-permute-start | bytes 196616 | tf_op jit(solution)/shard_map/reduce/ppermute | solution.py:250
  10.5 4.1 %collective-permute-start.1 = (f32[128,128]{1,0:T(8,128)S(1)}, f32[128,128]{1,0:T(8,128)S(1)}, u32[]{:S(2)}, u32[]{:S(2)}) collective-permute-start(f32[128,128]{1,0:T(8,128)S(1)} %slice_add_fusion.1), channel_id=1, source_target_pairs={{0,3},{1,0},{2,1},{3,2},{4,7},{5,4},{6,5},{7,6},{8,11},{9,8},{10,9... | collective-permute-start | bytes 196616 | tf_op jit(solution)/shard_map/reduce/ppermute | solution.py:258
  11.7 3.8 %collective-permute-start.3 = (f32[128,128]{1,0:T(8,128)S(1)}, f32[128,128]{1,0:T(8,128)S(1)}, u32[]{:S(2)}, u32[]{:S(2)}) collective-permute-start(f32[128,128]{1,0:T(8,128)S(1)} %slice_add_fusion), channel_id=1, source_target_pairs={{0,3},{1,0},{2,1},{3,2},{4,7},{5,4},{6,5},{7,6},{8,11},{9,8},{10,9... | collective-permute-start | bytes 196616 | tf_op jit(solution)/shard_map/reduce/ppermute | solution.py:258
  15.6 4.3 %collective-permute-start.7 = (f32[64,128]{1,0:T(8,128)S(1)}, f32[64,128]{1,0:T(8,128)S(1)}, u32[]{:S(2)}, u32[]{:S(2)}) collective-permute-start(f32[64,128]{1,0:T(8,128)S(1)} %pad_maximum_fusion.3), channel_id=1, source_target_pairs={{1,8},{0,1},{3,10},{2,3},{5,12},{4,5},{7,14},{6,7},{9,0},{8,9},{11... | collective-permute-start | bytes 98312 | tf_op jit(solution)/shard_map/reduce/ppermute | solution.py:258
  18.6 1.3 %collective-permute-start.6 = (f32[64,128]{1,0:T(8,128)S(1)}, f32[64,128]{1,0:T(8,128)S(1)}, u32[]{:S(2)}, u32[]{:S(2)}) collective-permute-start(f32[64,128]{1,0:T(8,128)S(1)} %pad_maximum_fusion.2), channel_id=1, source_target_pairs={{1,4},{0,1},{3,6},{2,3},{5,8},{4,5},{7,10},{6,7},{9,12},{8,9},{11,... | collective-permute-start | bytes 98312 | tf_op jit(solution)/shard_map/reduce/ppermute | solution.py:258
  18.6 2.3 %collective-permute-start.5 = (f32[64,128]{1,0:T(8,128)S(1)}, f32[64,128]{1,0:T(8,128)S(1)}, u32[]{:S(2)}, u32[]{:S(2)}) collective-permute-start(f32[64,128]{1,0:T(8,128)S(1)} %pad_maximum_fusion.1), channel_id=1, source_target_pairs={{1,12},{0,1},{3,14},{2,3},{5,0},{4,5},{7,2},{6,7},{9,4},{8,9},{11,... | collective-permute-start | bytes 98312 | tf_op jit(solution)/shard_map/reduce/ppermute | solution.py:258
  19.8 1.2 %collective-permute-start.4 = (f32[64,128]{1,0:T(8,128)S(1)}, f32[64,128]{1,0:T(8,128)S(1)}, u32[]{:S(2)}, u32[]{:S(2)}) collective-permute-start(f32[64,128]{1,0:T(8,128)S(1)} %pad_maximum_fusion), channel_id=1, source_target_pairs={{0,1},{1,0},{2,3},{3,2},{4,5},{5,4},{6,7},{7,6},{8,9},{9,8},{10,11... | collective-permute-start | bytes 98312 | tf_op jit(solution)/shard_map/reduce/ppermute | solution.py:250
  21.1 5.2 %collective-permute-start.8 = (f32[64,128]{1,0:T(8,128)S(1)}, f32[64,128]{1,0:T(8,128)S(1)}, u32[]{:S(2)}, u32[]{:S(2)}) collective-permute-start(f32[64,128]{1,0:T(8,128)S(1)} %add_add_fusion), channel_id=1, source_target_pairs={{0,19},{1,0},{2,17},{3,2},{4,23},{5,4},{6,21},{7,6},{8,27},{9,8},{... | collective-permute-start | bytes 98312 | tf_op jit(solution)/shard_map/gather/ppermute | solution.py:258
  22.5 3.7 %collective-permute-start.9 = (f32[64,128]{1,0:T(8,128)S(1)}, f32[64,128]{1,0:T(8,128)S(1)}, u32[]{:S(2)}, u32[]{:S(2)}) collective-permute-start(f32[64,128]{1,0:T(8,128)S(1)} %add_add_fusion), channel_id=1, source_target_pairs={{0,1},{1,0},{2,3},{3,2},{4,5},{5,4},{6,7},{7,6},{8,9},{9,8},{10,11... | collective-permute-start | bytes 98312 | tf_op jit(solution)/shard_map/gather/ppermute | solution.py:250
  26.3 3.6 %collective-permute-start.10 = (f32[128,128]{1,0:T(8,128)S(1)}, f32[128,128]{1,0:T(8,128)S(1)}, u32[]{:S(2)}, u32[]{:S(2)}) collective-permute-start(f32[128,128]{1,0:T(8,128)S(1)} %get-tuple-element.61), channel_id=1, source_target_pairs={{1,64},{0,1},{3,66},{2,3},{5,68},{4,5},{7,70},{6,7},{9,72},{8,9},{... | collective-permute-start | bytes 196616 | tf_op jit(solution)/shard_map/gather/ppermute | solution.py:258
  28.6 1.9 %collective-permute-start.11 = (f32[128,128]{1,0:T(8,128)S(1)}, f32[128,128]{1,0:T(8,128)S(1)}, u32[]{:S(2)}, u32[]{:S(2)}) collective-permute-start(f32[128,128]{1,0:T(8,128)S(1)} %get-tuple-element.61), channel_id=1, source_target_pairs={{1,32},{0,1},{3,34},{2,3},{5,36},{4,5},{7,38},{6,7},{9,40},{8,9},{... | collective-permute-start | bytes 196616 | tf_op jit(solution)/shard_map/gather/ppermute | solution.py:258
  28.6 2.5 %collective-permute-start.12 = (f32[128,128]{1,0:T(8,128)S(1)}, f32[128,128]{1,0:T(8,128)S(1)}, u32[]{:S(2)}, u32[]{:S(2)}) collective-permute-start(f32[128,128]{1,0:T(8,128)S(1)} %get-tuple-element.61), channel_id=1, source_target_pairs={{1,96},{0,1},{3,98},{2,3},{5,100},{4,5},{7,102},{6,7},{9,104},{8,9... | collective-permute-start | bytes 196616 | tf_op jit(solution)/shard_map/gather/ppermute | solution.py:258
  29.7 1.3 %collective-permute-start.13 = (f32[128,128]{1,0:T(8,128)S(1)}, f32[128,128]{1,0:T(8,128)S(1)}, u32[]{:S(2)}, u32[]{:S(2)}) collective-permute-start(f32[128,128]{1,0:T(8,128)S(1)} %get-tuple-element.61), channel_id=1, source_target_pairs={{0,1},{1,0},{2,3},{3,2},{4,5},{5,4},{6,7},{7,6},{8,9},{9,8},{10,11... | collective-permute-start | bytes 196616 | tf_op jit(solution)/shard_map/gather/ppermute | solution.py:250
  31.3 4.6 %collective-permute-start.14 = (f32[8,128]{1,0:T(8,128)S(1)}, f32[8,128]{1,0:T(8,128)S(1)}, u32[]{:S(2)}, u32[]{:S(2)}) collective-permute-start(f32[8,128]{1,0:T(8,128)S(1)} %gram.2), channel_id=1, source_target_pairs={{0,9},{1,0},{2,11},{3,2},{4,13},{5,4},{6,15},{7,6},{8,1},{9,8},{10... | collective-permute-start | bytes 12296 | tf_op jit(solution)/shard_map/gram/ppermute | solution.py:258
  33.1 4.2 %collective-permute-start.15 = (f32[8,128]{1,0:T(8,128)S(1)}, f32[8,128]{1,0:T(8,128)S(1)}, u32[]{:S(2)}, u32[]{:S(2)}) collective-permute-start(f32[8,128]{1,0:T(8,128)S(1)} %gram.2), channel_id=1, source_target_pairs={{0,5},{1,0},{2,7},{3,2},{4,9},{5,4},{6,11},{7,6},{8,13},{9,8},{10,... | collective-permute-start | bytes 12296 | tf_op jit(solution)/shard_map/gram/ppermute | solution.py:258
  33.2 4.2 %collective-permute-start.16 = (f32[8,128]{1,0:T(8,128)S(1)}, f32[8,128]{1,0:T(8,128)S(1)}, u32[]{:S(2)}, u32[]{:S(2)}) collective-permute-start(f32[8,128]{1,0:T(8,128)S(1)} %gram.2), channel_id=1, source_target_pairs={{0,13},{1,0},{2,15},{3,2},{4,1},{5,4},{6,3},{7,6},{8,5},{9,8},{10,... | collective-permute-start | bytes 12296 | tf_op jit(solution)/shard_map/gram/ppermute | solution.py:258
  33.7 3.6 %collective-permute-start.17 = (f32[8,128]{1,0:T(8,128)S(1)}, f32[8,128]{1,0:T(8,128)S(1)}, u32[]{:S(2)}, u32[]{:S(2)}) collective-permute-start(f32[8,128]{1,0:T(8,128)S(1)} %gram.2), channel_id=1, source_target_pairs={{0,1},{1,0},{2,3},{3,2},{4,5},{5,4},{6,7},{7,6},{8,9},{9,8},{10,11... | collective-permute-start | bytes 12296 | tf_op jit(solution)/shard_map/gram/ppermute | solution.py:250
  35.5 3.0 %collective-permute-start.21 = (f32[64,128]{1,0:T(8,128)S(1)}, f32[64,128]{1,0:T(8,128)S(1)}, u32[]{:S(2)}, u32[]{:S(2)}) collective-permute-start(f32[64,128]{1,0:T(8,128)S(1)} %get-tuple-element.47.here), channel_id=1, source_target_pairs={{0,2},{1,3},{2,0},{3,1},{4,6},{5,7},{6,4},{7,5},{8,10},{9,11},{10,... | collective-permute-start | bytes 98312 | tf_op jit(solution)/shard_map/gram/ppermute | solution.py:263
  37.3 2.7 %collective-permute-start.18 = (f32[8,128]{1,0:T(8,128)S(1)}, f32[8,128]{1,0:T(8,128)S(1)}, u32[]{:S(2)}, u32[]{:S(2)}) collective-permute-start(f32[8,128]{1,0:T(8,128)S(1)} %add_add_fusion.1), channel_id=1, source_target_pairs={{0,2},{1,3},{2,0},{3,1},{4,6},{5,7},{6,4},{7,5},{8,10},{9,11},{10,... | collective-permute-start | bytes 12296 | tf_op jit(solution)/shard_map/gram/ppermute | solution.py:263
  37.8 2.2 %collective-permute-start.19 = (f32[8,128]{1,0:T(8,128)S(1)}, f32[8,128]{1,0:T(8,128)S(1)}, u32[]{:S(2)}, u32[]{:S(2)}) collective-permute-start(f32[8,128]{1,0:T(8,128)S(1)} %add_add_fusion.1), channel_id=1, source_target_pairs={{1,2},{0,1},{3,0},{2,3},{5,6},{4,5},{7,4},{6,7},{9,10},{8,9},{11,8... | collective-permute-start | bytes 12296 | tf_op jit(solution)/shard_map/gram/ppermute | solution.py:258
  38.4 1.6 %collective-permute-start.20 = (f32[8,128]{1,0:T(8,128)S(1)}, f32[8,128]{1,0:T(8,128)S(1)}, u32[]{:S(2)}, u32[]{:S(2)}) collective-permute-start(f32[8,128]{1,0:T(8,128)S(1)} %add_add_fusion.1), channel_id=1, source_target_pairs={{0,1},{1,0},{2,3},{3,2},{4,5},{5,4},{6,7},{7,6},{8,9},{9,8},{10,11... | collective-permute-start | bytes 12296 | tf_op jit(solution)/shard_map/gram/ppermute | solution.py:250
